TPU v7x, 512 devices: a whole 4x8x8 slice. The times are simulated.
512 devices in a mesh: dp: 64 (over z, y_lo, core), tensor: 8 (over y_hi, x).
Axes of the slice: x: 4, y: 8 (y_hi: 2, y_lo: 4; y = y_hi * 4 + y_lo), z: 8, core: 2. Of those that a mesh axis runs over, the one named last changes fastest.
Arguments:
- calib_inputs: bfloat16 [49152, 16384], P('dp', 'tensor'), may hold values from -54 to 54, as said below
- weights: bfloat16 [53248, 4096], P(('dp', 'tensor')), may hold values from -6 to 6
- inverse_chol: float32 [256, 4096], P(None, 'dp'), may hold values from -0.3 to 2, as said below
- keep_pattern: int32 [53248, 64], P(('dp', 'tensor')), may hold values from 0 to 5
Outputs:
- pruned_weights: bfloat16 [53248, 4096], P(('dp', 'tensor'))
- gram_panel: float32 [256, 16384], P('dp', 'tensor')
Inputs may be any that keep to these rules, and one draw needn't show every extreme that they name: `calib_inputs`: each row (calibration token) and each feature carry their own scale. `inverse_chol`: zero below the diagonal (row j against window column j); the diagonal lies within 0.5 to 2.
All inputs are finite; a program needn't handle non-finite values.
Results may differ from a plain program's by a relative error of at most 0.001.
Values may be sent and summed in bfloat16 or wider, within the bound.
A program may use at most 64 MiB of HBM per device.

v0:
```python
import jax
import jax.numpy as jnp
import numpy as np
from jax import lax
from jax.sharding import PartitionSpec as P


def spread(value, axis, root):
    mine = lax.axis_index(axis) == root
    return lax.psum(jnp.where(mine, value, jnp.zeros_like(value)), axis)


def keep_columns(pattern_rows, panel_width):
    first_pos = jnp.array(np.array([0, 0, 0, 1, 1, 2]), dtype=jnp.int32)
    second_pos = jnp.array(np.array([1, 2, 3, 2, 3, 3]), dtype=jnp.int32)
    pattern_cols = jnp.repeat(pattern_rows, 4, axis=1)
    position = jnp.arange(panel_width, dtype=jnp.int32) % 4
    chosen = pattern_cols[:, :, None] == jnp.arange(6, dtype=jnp.int32)[None, None, :]
    first_sel = jnp.sum(jnp.where(chosen, first_pos[None, None, :], 0), axis=-1)
    second_sel = jnp.sum(jnp.where(chosen, second_pos[None, None, :], 0), axis=-1)
    hit = (position[None, :] == first_sel) | (position[None, :] == second_sel)
    return jnp.where(hit, 1.0, 0.0).astype(jnp.float32)


def sweep_step(column_at, carry, keep_cols, head_block, col_index):
    panel_cols, errors = carry
    column = lax.dynamic_slice_in_dim(panel_cols, column_at, 1, 1)[:, 0]
    keep_col = lax.dynamic_slice_in_dim(keep_cols, column_at, 1, 1)[:, 0]
    pruned_col = column * keep_col
    chol_row = lax.dynamic_slice_in_dim(head_block, column_at, 1, 0)[0]
    pivot_value = lax.dynamic_slice_in_dim(chol_row, column_at, 1, 0)[0]
    error_col = (column - pruned_col) / pivot_value
    row_after = jnp.where(col_index > column_at, chol_row, jnp.float32(0.0))
    panel_cols = panel_cols - error_col[:, None] * row_after[None, :]
    select = (col_index == column_at)[None, :]
    panel_cols = jnp.where(select, pruned_col[:, None], panel_cols)
    errors = jnp.where(select, error_col[:, None], errors)
    return (panel_cols, errors)


def sweep_panel(panel_cols, keep_cols, head_block):
    panel_width = head_block.shape[0]
    block_width = 32
    inner_width = 8
    block_index = jnp.arange(block_width, dtype=jnp.int32)
    error_parts = []
    for block_number in range(panel_width // block_width):
        start = block_number * block_width
        stop = start + block_width
        block_cols = panel_cols[:, start:stop]
        block_keep = keep_cols[:, start:stop]
        block_chol = head_block[start:stop, start:stop]

        def advance(outer_step, carry):
            for inner_step in range(inner_width):
                carry = sweep_step(
                    outer_step * inner_width + inner_step,
                    carry,
                    block_keep,
                    block_chol,
                    block_index,
                )
            return carry

        begin_state = (block_cols, jnp.zeros_like(block_cols))
        block_done, block_errors = lax.fori_loop(
            0, block_width // inner_width, advance, begin_state
        )
        error_parts.append(block_errors)
        if stop < panel_width:
            later_cols = panel_cols[:, stop:] - jnp.dot(
                block_errors,
                head_block[start:stop, stop:],
                precision=lax.Precision.HIGHEST,
                preferred_element_type=jnp.float32,
            )
            panel_cols = jnp.concatenate([panel_cols[:, :start], block_done, later_cols], axis=1)
        else:
            panel_cols = jnp.concatenate([panel_cols[:, :start], block_done], axis=1)
    return (panel_cols, jnp.concatenate(error_parts, axis=1))


def shards(calib_inputs, weights, inverse_chol, keep_pattern):
    panel_width = inverse_chol.shape[0]
    feat_dev = calib_inputs.shape[1]
    full_feat = feat_dev * lax.axis_size("tensor")
    window = weights.shape[1]
    window_start = full_feat - window
    owner_rank = window_start // feat_dev
    offset = window_start % feat_dev
    local_panel = calib_inputs[:, offset : offset + panel_width]
    panel_inputs = spread(local_panel, "tensor", owner_rank)
    tokens_all = calib_inputs.shape[0] * lax.axis_size("dp")
    gram_rows = lax.psum_scatter(
        lax.dot_general(
            panel_inputs, calib_inputs, (((0,), (0,)), ((), ())), preferred_element_type=jnp.float32
        ),
        "dp",
        scatter_dimension=0,
        tiled=True,
    )
    gram_panel = gram_rows * (2.0 / tokens_all)
    inverse_full = lax.all_gather(inverse_chol, "dp", axis=1, tiled=True)
    weight_f32 = weights.astype(jnp.float32)
    keep_cols = keep_columns(keep_pattern, panel_width)
    head_block = inverse_full[:, :panel_width]
    panel_cols, errors = sweep_panel(weight_f32[:, :panel_width], keep_cols, head_block)
    tail_cols = weight_f32[:, panel_width:] - jnp.dot(
        errors,
        inverse_full[:, panel_width:],
        precision=lax.Precision.HIGHEST,
        preferred_element_type=jnp.float32,
    )
    pruned_weights = jnp.concatenate([panel_cols, tail_cols], axis=1).astype(jnp.bfloat16)
    return (pruned_weights, gram_panel)


def solution(mesh):
    placed = (
        P("dp", "tensor"),
        P(("dp", "tensor"), None),
        P(None, "dp"),
        P(("dp", "tensor"), None),
    )
    return jax.shard_map(
        shards,
        mesh=mesh,
        in_specs=placed,
        out_specs=(P(("dp", "tensor"), None), P("dp", "tensor")),
        check_vma=False,
    )
```

profile of v0, /device:TPU:1, one launch (start us, length us, event | category | flops | bytes accessed | tf_op | source)
XLA Modules:
  0.0 1049.3 jit_solution(5088336196278209752)
XLA Ops:
  7.2 1.8 slice_select_fusion
  9.1 115.3 %all-reduce.4.cloned.1.call-done = bf16[768,256]{1,0:T(8,128)(2,1)} async-done(((bf16[768,256]{1,0:T(8,128)(2,1)}), bf16[768,256]{1,0:T(8,128)(2,1)}) %all-reduce.4.cloned.1.call-update) | async-done | bytes 393232 | tf_op jit(solution)/shard_map/psum | solution.py:10
  124.4 4.4 fusion.411
  131.0 1.3 dynamic-slice.448
  133.0 542.4 %all-reduce.6.cloned.1.call-done = f32[256,2048]{1,0:T(8,128)} async-done(((f32[256,2048]{1,0:T(8,128)}), f32[256,2048]{1,0:T(8,128)}) %all-reduce.6.cloned.1.call-update) | async-done | bytes 2097168
  675.3 1.5 dynamic-slice_multiply_fusion
  676.8 120.4 %all-gather.2.cloned.1.call-done = f32[256,4096]{0,1:T(8,128)} async-done(((f32[256,64]{0,1:T(8,128)}), f32[256,4096]{0,1:T(8,128)}) %all-gather.2.cloned.1.call-update) | async-done | bytes 4194320 | tf_op jit(solution)/shard_map/all_gather | solution.py:103
  797.2 0.9 fusion.409
  798.2 28.0 %while.160 = (s32[]{:T(128)}, f32[104,32]{0,1:T(8,128)S(1)}, f32[104,32]{0,1:T(8,128)S(1)}, f32[104,32]{0,1:T(8,128)S(1)}, f32[32,32]{1,0:T(8,128)S(1)}, /*index...) while((s32[]{:T(128)}, f32[104,32]{0,1:T(8,128)S(1)}, ...), condition=%wide.region_3.4_spmd.clone.clone, body=%wide.region_2.3_spmd.clone.clone.sunk | while | flops 392683 | bytes 295495 | solution.py:66
  826.2 1.3 convolution_subtract_fusion.3
  827.6 28.3 %while.161 = (s32[]{:T(128)}, f32[104,32]{0,1:T(8,128)S(1)}, f32[104,32]{0,1:T(8,128)S(1)}, f32[104,32]{0,1:T(8,128)S(1)}, f32[32,32]{1,0:T(8,128)S(1)}, /*index...) while((s32[]{:T(128)}, f32[104,32]{0,1:T(8,128)S(1)}, ...), condition=%wide.region_5.6_spmd.clone.clone, body=%wide.region_4.5_spmd.clone.clone.sunk | while | flops 392683 | bytes 295495 | solution.py:66
  848.9 0.7 fusion.522
  855.9 1.3 convolution_subtract_fusion.2
  857.4 28.3 %while.162 = (s32[]{:T(128)}, f32[104,32]{0,1:T(8,128)S(1)}, f32[104,32]{0,1:T(8,128)S(1)}, f32[104,32]{0,1:T(8,128)S(1)}, f32[32,32]{1,0:T(8,128)S(1)}, /*index...) while((s32[]{:T(128)}, f32[104,32]{0,1:T(8,128)S(1)}, ...), condition=%wide.region_7.8_spmd.clone.clone, body=%wide.region_6.7_spmd.clone.clone.sunk | while | flops 392683 | bytes 295495 | solution.py:66
  871.6 0.7 fusion.533
  878.7 0.7 fusion.533
  885.8 1.3 convolution_subtract_fusion.1
  887.2 28.3 %while.163 = (s32[]{:T(128)}, f32[104,32]{0,1:T(8,128)S(1)}, f32[104,32]{0,1:T(8,128)S(1)}, f32[104,32]{0,1:T(8,128)S(1)}, f32[32,32]{1,0:T(8,128)S(1)}, /*index...) while((s32[]{:T(128)}, f32[104,32]{0,1:T(8,128)S(1)}, ...), condition=%wide.region_9.10_spmd.clone.clone, body=%wide.region_8.9_spmd.clone.clone.sunk | while | flops 392683 | bytes 295495 | solution.py:66
  887.2 0.7 fusion.544
  894.3 0.7 fusion.544
  908.5 0.7 fusion.544
  915.5 1.2 convolution_subtract_fusion.7
  916.8 28.3 %while.164 = (s32[]{:T(128)}, f32[104,32]{0,1:T(8,128)S(1)}, f32[104,32]{0,1:T(8,128)S(1)}, f32[104,32]{0,1:T(8,128)S(1)}, f32[32,32]{1,0:T(8,128)S(1)}, /*index...) while((s32[]{:T(128)}, f32[104,32]{0,1:T(8,128)S(1)}, ...), condition=%wide.region_11.12_spmd.clone.clone, body=%wide.region_10.11_spmd.clone.clone.sunk | while | flops 392683 | bytes 295495 | solution.py:66
  916.9 0.7 fusion.555
  945.2 1.1 convolution_subtract_fusion.6
  946.4 28.3 %while.165 = (s32[]{:T(128)}, f32[104,32]{0,1:T(8,128)S(1)}, f32[104,32]{0,1:T(8,128)S(1)}, f32[104,32]{0,1:T(8,128)S(1)}, f32[32,32]{1,0:T(8,128)S(1)}, /*index...) while((s32[]{:T(128)}, f32[104,32]{0,1:T(8,128)S(1)}, ...), condition=%wide.region_13.14_spmd.clone.clone, body=%wide.region_12.13_spmd.clone.clone.sunk | while | flops 392683 | bytes 295495 | solution.py:66
  974.8 1.1 convolution_subtract_fusion.5
  976.0 28.3 %while.166 = (s32[]{:T(128)}, f32[104,32]{0,1:T(8,128)S(1)}, f32[104,32]{0,1:T(8,128)S(1)}, f32[104,32]{0,1:T(8,128)S(1)}, f32[32,32]{1,0:T(8,128)S(1)}, /*index...) while((s32[]{:T(128)}, f32[104,32]{0,1:T(8,128)S(1)}, ...), condition=%wide.region_15.16_spmd.clone.clone, body=%wide.region_14.15_spmd.clone.clone.sunk | while | flops 392683 | bytes 295495 | solution.py:66
  1004.3 1.0 convolution_subtract_fusion.4
  1005.5 28.5 %while.167 = (s32[]{:T(128)}, f32[104,32]{0,1:T(8,128)S(1)}, f32[104,32]{0,1:T(8,128)S(1)}, f32[104,32]{0,1:T(8,128)S(1)}, f32[32,32]{1,0:T(8,128)S(1)}, /*index...) while((s32[]{:T(128)}, f32[104,32]{0,1:T(8,128)S(1)}, ...), condition=%wide.region_17.18_spmd.clone.clone, body=%wide.region_16.17_spmd.clone.clone.sunk | while | flops 392683 | bytes 295495 | solution.py:66
  1035.0 6.0 fusion.392
  1041.0 1.7 concatenate.8
  (810 shorter events, 218.4 us)
Async XLA Ops:
  7.2 117.3 %all-reduce.4.cloned.1.call-start = ((), (), s32[]{:S(2)}) async-start(), calls=%async_computation.1 | async-start | bytes 786432 | tf_op jit(solution)/shard_map/psum | solution.py:10
  9.0 120.6 %copy-start = (bf16[104,4096]{1,0:T(8,128)(2,1)S(1)}, bf16[104,4096]{1,0:T(8,128)(2,1)}, u32[]{:S(2)}) copy-start(bf16[104,4096]{1,0:T(8,128)(2,1)} %param.23) | copy-start | bytes 2555908
  9.0 120.8 %copy-start.1 = (s32[104,64]{0,1:T(8,128)S(1)}, s32[104,64]{0,1:T(8,128)}, u32[]{:S(2)}) copy-start(s32[104,64]{0,1:T(8,128)} %param.25) | copy-start | bytes 79876
  9.0 121.0 %copy-start.2 = (s32[6]{0:T(128)S(1)}, s32[6]{0:T(128)}, u32[]{:S(2)}) copy-start(s32[6]{0:T(128)} %constant.3924.clone) | copy-start | bytes 76
  9.0 121.0 %copy-start.3 = (s32[6]{0:T(128)S(1)}, s32[6]{0:T(128)}, u32[]{:S(2)}) copy-start(s32[6]{0:T(128)} %constant.3925.clone) | copy-start | bytes 76
  9.1 666.3 %all-reduce.6.cloned.1.call-start = ((), (), s32[]{:S(2)}) async-start(), calls=%async_computation.2 | async-start | bytes 4194304
  128.8 668.4 %all-gather.2.cloned.1.call-start = ((), (), s32[]{:S(2)}) async-start(), calls=%async_computation | async-start | bytes 4259840 | tf_op jit(solution)/shard_map/all_gather | solution.py:103
Sparse Core Ops, SparseCore 0:
  11.5 112.9 all-reduce.3
  128.9 546.3 all-reduce.5
  677.5 119.6 all-gather.1
where the time goes:
time: 1050 us
  waiting for transfers between devices  779 us (74%)
  other arithmetic  201 us (19%)
  local copies, waits for them, and re-layouts  28.9 us (3%)
  matrix products  18.5 us (2%)
  between operations  14.9 us (1%)
    unnamed x4, waiting for transfers between devices  543 us
    broadcast_in_dim x256, other arithmetic, sweep_step(): panel_cols = jnp.where(select, pruned_col[:, None], panel_cols)  163 us
    all_gather x1, waiting for transfers between devices, shards(): inverse_full = lax.all_gather(inverse_chol, 'dp', axis=1, tiled=True)  120 us
    psum x1, waiting for transfers between devices, spread(): return lax.psum(jnp.where(mine, value, jnp.zeros_like(value)), axis)  115 us
    select_n x256, other arithmetic, sweep_step(): panel_cols = jnp.where(select, pruned_col[:, None], panel_cols)  28.9 us
    dynamic_slice x32, local copies, waits for them, and re-layouts, sweep_step(): pivot_value = lax.dynamic_slice_in_dim(chol_row, column_at, 1, 0)[0]  22.1 us
  transfers between devices with their start and end apart: 3, of which 3 were waited for; matrix products, arithmetic and copies ran while one was open for 0% of the time, Pallas kernels for 0%

commit v1 on v0

v1 whole, which is shorter than its diff:
```python
import jax
import jax.numpy as jnp
from jax import lax
from jax.experimental import pallas as pl
from jax.experimental.pallas import tpu as pltpu
from jax.sharding import PartitionSpec as P

MESH = pl.DeviceIdType.MESH
NZ, NY, NC, NH, NX = 8, 4, 2, 2, 4
PANEL_W = 256
WINDOW = 4096
ROWS = 104
LANES = 128
FEAT = 2048
TOK = 768
QTOK = TOK // NX
PART = PANEL_W // (NX * NC)
OWNER_X, OWNER_H = 2, 1
BLOCK = 32
CODE_MAX = 32767.0
CHOL_MAX = 2.0
SUM_MAX = 32000.0
F32 = jnp.float32
BF16 = jnp.bfloat16
HIGHEST = lax.Precision.HIGHEST


def contract(a, b, da, db, precision=None):
    return lax.dot_general(
        a, b, (((da,), (db,)), ((), ())), precision=precision, preferred_element_type=F32
    )


def identity(n, dtype):
    rows = lax.broadcasted_iota(jnp.int32, (n, n), 0)
    cols = lax.broadcasted_iota(jnp.int32, (n, n), 1)
    return jnp.where(rows == cols, 1.0, 0.0).astype(dtype)


def panel_order():
    rows = lax.broadcasted_iota(jnp.int32, (PANEL_W, PANEL_W), 0)
    cols = lax.broadcasted_iota(jnp.int32, (PANEL_W, PANEL_W), 1)
    core, rest = rows // 128, rows % 128
    feature = (rest // 4) * 8 + core * 4 + rest % 4
    return jnp.where(feature == cols, 1.0, 0.0).astype(BF16)


def encode_chol(value):
    root = jnp.sqrt(jnp.minimum(jnp.abs(value) * (1.0 / CHOL_MAX), 1.0)) * CODE_MAX
    code = jnp.round(jnp.where(value < 0.0, -root, root))
    return code.astype(jnp.int32).astype(jnp.int16)


def decode_chol(code):
    value = code.astype(jnp.int32).astype(F32)
    return value * jnp.abs(value) * (CHOL_MAX / (CODE_MAX * CODE_MAX))


def kernel(
    calib, weights, inverse, pattern,
    pruned, gram,
    xv, pv, wv, kv, iv, ipeer, qv, hv, gv, gpeer, msend, mrecv, ysend, yrecv,
    wpad, kpad, dg, ct, av, et, eh, el, pt,
    lsem, isem, s1s, s1r, s2s, s2r, qzs, qzr, qys, qyr, qxs, qxr, hzs, hzr, hys, hyr, hxs, hxr,
    ccs, ccr, gcs, gcr, rzs, rzr, rys, ryr,
):
    d = lax.axis_index("dp")
    t = lax.axis_index("tensor")
    z, y, c = d // (NY * NC), (d // NC) % NY, d % NC
    h, x = t // NX, t % NX
    owner = (h == OWNER_H) & (x == OWNER_X)

    def at(z=z, y=y, c=c, h=h, x=x):
        return ((z * NY + y) * NC + c, h * NX + x)

    def remote(src, dst, send, recv, where):
        return pltpu.make_async_remote_copy(
            src_ref=src, dst_ref=dst, send_sem=send, recv_sem=recv,
            device_id=where, device_id_type=MESH,
        )

    def zp(k):
        return lax.rem(z + k, NZ)

    def yp(k):
        return lax.rem(y + k, NY)

    def xp(k):
        return lax.rem(x + k, NX)

    load_i = pltpu.make_async_copy(inverse, iv, lsem.at[0])
    load_x = pltpu.make_async_copy(calib, xv, lsem.at[1])
    load_w = pltpu.make_async_copy(weights, wv, lsem.at[2])
    load_k = pltpu.make_async_copy(pattern, kv, lsem.at[3])
    load_p = pltpu.make_async_copy(calib.at[:, pl.ds(0, PANEL_W)], pv, lsem.at[4])
    load_i.start()
    pl.when(owner)(load_p.start)
    load_x.start()
    load_w.start()
    load_k.start()

    barrier = pltpu.get_barrier_semaphore()
    partners = [at(c=1 - c)]
    partners += [at(z=zp(k)) for k in range(1, NZ)]
    partners += [at(y=yp(k)) for k in range(1, NY)]
    partners += [at(x=xp(k)) for k in range(1, NX)]
    partners += [at(h=1 - h, x=xp(k)) for k in range(NX)]
    for partner in partners:
        pl.semaphore_signal(barrier, inc=1, device_id=partner, device_id_type=MESH)
    pl.semaphore_wait(barrier, len(partners))

    scatter = []
    for k in range(1, NH * NX):
        td = lax.rem(t + k, NH * NX)
        rows = pl.ds(pl.multiple_of(lax.rem(td, NX) * QTOK, QTOK), QTOK)
        scatter.append(
            remote(calib.at[rows, pl.ds(0, PANEL_W)], pv.at[rows], s1s.at[k - 1], s1r.at[0], (d, td))
        )

    @pl.when(owner)
    def _():
        for copy in scatter:
            copy.start()

    load_i.wait()
    pair = remote(iv, ipeer, isem.at[0], isem.at[1], at(c=1 - c))
    pair.start()

    my_quarter = pl.ds(pl.multiple_of(x * QTOK, QTOK), QTOK)
    part_at = pl.multiple_of(c * 128 + x * PART, PART)
    part = pl.ds(part_at, PART)
    half = pl.ds(pl.multiple_of(c * 128, 128), 128)

    pair.wait_recv()
    mine = iv[part, :]
    peers = ipeer[part, :]
    even = jnp.full(mine.shape, c, jnp.int32) == 0
    block = jnp.concatenate([jnp.where(even, mine, peers), jnp.where(even, peers, mine)], axis=1)
    my_cols = pl.ds(pl.multiple_of(z * 128, 128), 128)
    qv[y, part, my_cols] = encode_chol(block)
    head_chip = (z == 0) & (y < 2)
    head_line = y < 2
    hy = jnp.minimum(y, 1)

    @pl.when(head_chip)
    def _():
        hv[hy, part, :] = block

    q_z = [
        remote(qv.at[y, part, my_cols], qv.at[y, part, my_cols], qzs.at[k - 1], qzr.at[k - 1], at(z=zp(k)))
        for k in range(1, NZ)
    ]
    h_z = [
        remote(hv.at[hy, part], hv.at[hy, part], hzs.at[k - 1], hzr.at[0], at(z=zp(k)))
        for k in range(1, NZ)
    ]

    @pl.when(head_chip)
    def _():
        for copy in h_z:
            copy.start()

    for copy in q_z:
        copy.start()

    @pl.when(owner)
    def _():
        load_p.wait()

    @pl.when(jnp.logical_not(owner))
    def _():
        remote(pv.at[my_quarter], pv.at[my_quarter], s1s.at[0], s1r.at[0], at(c=1 - c)).wait_recv()

    share = []
    for k in range(1, NX):
        to_owner = (h == OWNER_H) & (xp(k) == OWNER_X)
        copy = remote(pv.at[my_quarter], pv.at[my_quarter], s2s.at[k - 1], s2r.at[k - 1], at(x=xp(k)))
        pl.when(jnp.logical_not(to_owner))(copy.start)
        share.append((copy, to_owner))

    for k in range(1, NZ):
        cols = pl.ds(pl.multiple_of(zp(NZ - k) * 128, 128), 128)
        remote(qv.at[y, part, cols], qv.at[y, part, cols], qzs.at[k - 1], qzr.at[k - 1], at(z=zp(k))).wait_recv()

    @pl.when(head_line & (z > 0))
    def _():
        h_z[0].wait_recv()

    h_y = [
        remote(hv.at[hy, part], hv.at[hy, part], hys.at[k - 1], hyr.at[k - 1], at(y=yp(k)))
        for k in range(1, NY)
    ]

    @pl.when(head_line)
    def _():
        for copy in h_y:
            copy.start()

    q_y = [
        remote(qv.at[y, part], qv.at[y, part], qys.at[k - 1], qyr.at[k - 1], at(y=yp(k)))
        for k in range(1, NY)
    ]
    for copy in q_y:
        copy.start()

    for k in range(1, NX):
        rows = pl.ds(pl.multiple_of(xp(NX - k) * QTOK, QTOK), QTOK)

        @pl.when(jnp.logical_not(owner))
        def _():
            remote(pv.at[rows], pv.at[rows], s2s.at[k - 1], s2r.at[k - 1], at(x=xp(k))).wait_recv()

    load_x.wait()
    pt[...] = contract(panel_order(), pv[...], 1, 1).astype(BF16)
    g_c = []
    for tile in range(4):
        cols = slice(tile * 512, tile * 512 + 512)
        gv[tile] = contract(pt[...], xv[:, cols], 1, 0).reshape(2, 128, 512)
        copy = remote(gv.at[tile, 1 - c], gpeer.at[tile], gcs.at[tile], gcr.at[tile], at(c=1 - c))
        copy.start()
        g_c.append(copy)

    for k in range(1, NY):
        yo = yp(NY - k)
        remote(qv.at[yo, part], qv.at[yo, part], qys.at[k - 1], qyr.at[k - 1], at(y=yp(k))).wait_recv()
        ho = jnp.minimum(yo, 1)

        @pl.when(yo < 2)
        def _():
            remote(hv.at[ho, part], hv.at[ho, part], hys.at[k - 1], hyr.at[k - 1], at(y=yp(k))).wait_recv()

    h_x = [remote(hv.at[:, part], hv.at[:, part], hxs.at[k - 1], hxr.at[k - 1], at(x=xp(k))) for k in range(1, NX)]
    q_x = [remote(qv.at[:, part], qv.at[:, part], qxs.at[k - 1], qxr.at[k - 1], at(x=xp(k))) for k in range(1, NX)]
    for copy in h_x + q_x:
        copy.start()

    for copy in g_c:
        copy.wait_recv()

    def pack(k, carry):
        zd = lax.rem(z + k, NZ)
        rows = pl.ds(pl.multiple_of(zd * 16, 16), 16)
        parts = [gv[tile, c, rows, :] + gpeer[tile, rows, :] for tile in range(4)]
        for tile in range(4):
            gpeer[tile, rows, :] = parts[tile]
        tiles = [p[:, 128 * i : 128 * i + 128] for p in parts for i in range(4)]
        most = jnp.abs(tiles[0])
        for value in tiles[1:]:
            most = jnp.maximum(most, jnp.abs(value))
        most = jnp.max(most, axis=0, keepdims=True)
        power = jnp.ceil(jnp.log2(jnp.maximum(most, 1e-30)))
        up = jnp.exp2(-power) * SUM_MAX
        for i, value in enumerate(tiles):
            msend[zd, i] = jnp.round(value * up).astype(jnp.int32).astype(jnp.int16)
        msend[zd, 16] = jnp.broadcast_to(power, (16, 128)).astype(jnp.int32).astype(jnp.int16)
        return carry

    lax.fori_loop(0, NZ, pack, 0)
    r_z = [
        remote(msend.at[zp(k)], mrecv.at[k - 1], rzs.at[k - 1], rzr.at[k - 1], at(z=zp(k)))
        for k in (4, 3, 5, 2, 6, 1, 7)
    ]
    for copy in r_z:
        copy.start()

    load_w.wait()
    load_k.wait()
    wpad[...] = jnp.zeros_like(wpad)
    wpad[0:ROWS, :] = wv[:, 0:PANEL_W].astype(F32)
    kpad[...] = jnp.zeros_like(kpad)
    kpad[0:ROWS, 0:64] = kv[...].astype(F32)
    ct[...] = contract(identity(PANEL_W, BF16), wpad[...].astype(BF16), 1, 1)
    col_id = lax.broadcasted_iota(jnp.int32, (PANEL_W, LANES), 0)
    group_id = lax.broadcasted_iota(jnp.int32, (PANEL_W, LANES), 1)
    repeat = jnp.where(col_id // 4 == group_id, 1.0, 0.0).astype(BF16)
    choice = contract(repeat, kpad[...].astype(BF16), 1, 1).astype(jnp.int32)
    place = col_id % 4
    drop = (
        ((place == 0) & (choice >= 3))
        | ((place == 1) & ((choice == 1) | (choice == 2) | (choice == 5)))
        | ((place == 2) & ((choice == 0) | (choice == 2) | (choice == 4)))
        | ((place == 3) & ((choice == 0) | (choice == 1) | (choice == 3)))
    )

    for k in range(1, NX):
        rows = pl.ds(pl.multiple_of(c * 128 + xp(NX - k) * PART, PART), PART)
        remote(hv.at[:, rows], hv.at[:, rows], hxs.at[k - 1], hxr.at[k - 1], at(x=xp(k))).wait_recv()
    other = pl.ds(pl.multiple_of((1 - c) * 128, 128), 128)
    h_c = remote(hv.at[:, half], hv.at[:, half], ccs.at[0], ccr.at[0], at(c=1 - c))
    h_c.start()
    remote(hv.at[:, other], hv.at[:, other], ccs.at[0], ccr.at[0], at(c=1 - c)).wait_recv()

    head = jnp.concatenate([hv[0], hv[1]], axis=1)
    row_id = lax.broadcasted_iota(jnp.int32, (PANEL_W, PANEL_W), 0)
    lane_id = lax.broadcasted_iota(jnp.int32, (PANEL_W, PANEL_W), 1)
    pivot = jnp.sum(jnp.where(row_id == lane_id, head, 0.0), axis=1, keepdims=True)
    av[...] = jnp.where(drop, jnp.broadcast_to(1.0 / pivot, (PANEL_W, LANES)), 0.0)
    upper = jnp.where(lane_id > row_id, head, 0.0).T
    for b in range(PANEL_W // BLOCK):
        at_b = b * BLOCK
        dg[b, :, 0:BLOCK] = upper[at_b : at_b + BLOCK, at_b : at_b + BLOCK]

    def sweep(b, carry):
        rows = pl.ds(pl.multiple_of(b * BLOCK, BLOCK), BLOCK)
        factor = av[rows, :]
        corner = dg[b]
        now = ct[rows, :]
        cols = [now[8 * v : 8 * v + 8, :] for v in range(BLOCK // 8)]
        for j in range(BLOCK):
            v0 = j // 8
            err = cols[v0][j % 8 : j % 8 + 1, :] * factor[j : j + 1, :]
            for v in range(v0, BLOCK // 8):
                cols[v] = cols[v] - corner[8 * v : 8 * v + 8, j : j + 1] * err
        done = jnp.concatenate(cols, axis=0)
        errors = done * factor
        et[rows, :] = errors
        chol_rows = jnp.concatenate([hv[0, rows, :], hv[1, rows, :]], axis=1)
        update = contract(chol_rows, errors, 0, 0, HIGHEST)
        later = col_id >= (b + 1) * BLOCK
        ct[...] = ct[...] - jnp.where(later, update, 0.0)
        ct[rows, :] = done
        return carry

    lax.fori_loop(0, PANEL_W // BLOCK, sweep, 0)
    kept = jnp.where(drop, 0.0, ct[...]).astype(BF16)
    eye = identity(PANEL_W, BF16)
    kept_rows = contract(kept, eye, 0, 0)
    errors = et[...]
    errors_hi = errors.astype(BF16)
    errors_lo = (errors - errors_hi.astype(F32)).astype(BF16)
    eh[...] = contract(errors_hi, eye, 0, 0).astype(BF16)
    el[...] = contract(errors_lo, eye, 0, 0).astype(BF16)

    for k in range(1, NX):
        rows = pl.ds(pl.multiple_of(c * 128 + xp(NX - k) * PART, PART), PART)
        remote(qv.at[:, rows], qv.at[:, rows], qxs.at[k - 1], qxr.at[k - 1], at(x=xp(k))).wait_recv()
    q_c = remote(qv.at[:, half], qv.at[:, half], ccs.at[1], ccr.at[1], at(c=1 - c))
    q_c.start()

    for k in range(1, NZ):
        remote(msend.at[zp(k)], mrecv.at[k - 1], rzs.at[k - 1], rzr.at[k - 1], at(z=zp(k))).wait_recv()
    own = pl.ds(pl.multiple_of(z * 16, 16), 16)

    for tile in range(4):
        def collect(k, total):
            down = jnp.exp2(mrecv[k, 16].astype(jnp.int32).astype(F32)) * (1.0 / SUM_MAX)
            pieces = [
                mrecv[k, tile * 4 + i].astype(jnp.int32).astype(F32) * down for i in range(4)
            ]
            return total + jnp.concatenate(pieces, axis=1)

        gpeer[tile, own, :] = lax.fori_loop(0, NZ - 1, collect, gpeer[tile, own, :])
    for tile in range(4):
        summed = gpeer[tile, own, :]
        for yd in range(NY):
            ysend[yd, tile * 4 : tile * 4 + 4, :] = summed[yd * 4 : yd * 4 + 4, :]
    r_y = [
        remote(ysend.at[yp(k)], yrecv.at[k - 1], rys.at[k - 1], ryr.at[k - 1], at(y=yp(k)))
        for k in range(1, NY)
    ]
    for copy in r_y:
        copy.start()

    remote(qv.at[:, other], qv.at[:, other], ccs.at[1], ccr.at[1], at(c=1 - c)).wait_recv()

    def tail(step, carry):
        yq, zq = step // 4, (step % 4) * 2
        code = qv[yq, :, pl.ds(pl.multiple_of(zq * 128, 256), 256)]
        chol = decode_chol(code)
        chol_hi = chol.astype(BF16)
        chol_lo = (chol - chol_hi.astype(F32)).astype(BF16)
        update = contract(eh[...], chol_hi, 1, 0) + (
            contract(eh[...], chol_lo, 1, 0) + contract(el[...], chol_hi, 1, 0)
        )
        for i in range(2):
            cols = pl.ds(pl.multiple_of(((zq + i) * 4 + yq) * 128, 128), 128)
            pruned[:, cols] = (
                wv[:, cols].astype(F32) - update[0:ROWS, 128 * i : 128 * i + 128]
            ).astype(BF16)
        return carry

    lax.fori_loop(0, 16, tail, 0)
    pruned[:, 0:PANEL_W] = kept_rows[0:ROWS, :].astype(BF16)

    for copy in r_y:
        copy.wait_recv()
    total = ysend[y] + yrecv[0] + yrecv[1] + yrecv[2]
    total = total * (2.0 / (TOK * NZ * NY * NC))
    for tile in range(4):
        gram[:, tile * 512 : tile * 512 + 512] = total[tile * 4 : tile * 4 + 4, :]

    @pl.when(owner)
    def _():
        for copy in scatter:
            copy.wait_send()

    @pl.when(head_chip)
    def _():
        for copy in h_z:
            copy.wait_send()

    @pl.when(head_line)
    def _():
        for copy in h_y:
            copy.wait_send()

    for copy, to_owner in share:
        pl.when(jnp.logical_not(to_owner))(copy.wait_send)
    for copy in [pair] + q_z + q_y + h_x + q_x + g_c + r_z + [h_c, q_c] + r_y:
        copy.wait_send()


def shards(calib_inputs, weights, inverse_chol, keep_pattern):
    dma = pltpu.SemaphoreType.DMA
    vmem = pltpu.VMEM
    scratch = [
        vmem((TOK, FEAT), BF16),
        vmem((TOK, PANEL_W), BF16),
        vmem((ROWS, WINDOW), BF16),
        vmem((ROWS, 64), jnp.int32),
        vmem((PANEL_W, 64), F32),
        vmem((PANEL_W, 64), F32),
        vmem((NY, PANEL_W, NZ * 128), jnp.int16),
        vmem((2, PANEL_W, 128), F32),
        vmem((4, 2, 128, 512), F32),
        vmem((4, 128, 512), F32),
        vmem((NZ, 17, 16, 128), jnp.int16),
        vmem((NZ - 1, 17, 16, 128), jnp.int16),
        vmem((NY, 16, 512), F32),
        vmem((NY - 1, 16, 512), F32),
        vmem((LANES, PANEL_W), F32),
        vmem((LANES, LANES), F32),
        vmem((PANEL_W // BLOCK, BLOCK, 128), F32),
        vmem((PANEL_W, LANES), F32),
        vmem((PANEL_W, LANES), F32),
        vmem((PANEL_W, LANES), F32),
        vmem((LANES, PANEL_W), BF16),
        vmem((LANES, PANEL_W), BF16),
        vmem((PANEL_W, TOK), BF16),
    ]
    sems = [5, 2, 7, 1, 3, 3, 7, 7, 3, 3, 3, 3, 7, 1, 3, 3, 3, 3, 2, 2, 4, 4, 7, 7, 3, 3]
    scratch += [dma((n,)) for n in sems]
    anywhere = pl.BlockSpec(memory_space=pl.ANY)
    inside = pl.BlockSpec(memory_space=pltpu.VMEM)
    return pl.pallas_call(
        kernel,
        out_shape=(
            jax.ShapeDtypeStruct((ROWS, WINDOW), BF16),
            jax.ShapeDtypeStruct((PANEL_W // (NZ * NY * NC), FEAT), F32),
        ),
        in_specs=[anywhere] * 4,
        out_specs=(inside, inside),
        scratch_shapes=scratch,
        compiler_params=pltpu.CompilerParams(
            collective_id=0, has_side_effects=True, vmem_limit_bytes=40 * 2**20
        ),
        cost_estimate=pl.CostEstimate(flops=2 * 10**9, bytes_accessed=8 * 10**6, transcendentals=0),
    )(calib_inputs, weights, inverse_chol, keep_pattern)


def solution(mesh):
    placed = (
        P("dp", "tensor"),
        P(("dp", "tensor"), None),
        P(None, "dp"),
        P(("dp", "tensor"), None),
    )
    return jax.shard_map(
        shards,
        mesh=mesh,
        in_specs=placed,
        out_specs=(P(("dp", "tensor"), None), P("dp", "tensor")),
        check_vma=False,
    )
```

time: 1050 us -> 75 us (0.07)
  waiting for transfers between devices: 779 us -> 0 us
  other arithmetic: 201 us -> 0 us
  Pallas kernels: 0 us -> 67.7 us
  local copies, waits for them, and re-layouts: 28.9 us -> 6.34 us
  matrix products: 18.5 us -> 0 us
  between operations: 14.9 us -> 0.66 us
    unnamed x4 -> x0, waiting for transfers between devices: 543 us -> none
    broadcast_in_dim x256 -> x0, other arithmetic: 163 us -> none  [sweep_step(): panel_cols = jnp.where(select, pruned_col[:, None], panel_cols)]
    all_gather x1 -> x0, waiting for transfers between devices: 120 us -> none  [shards(): inverse_full = lax.all_gather(inverse_chol, 'dp', axis=1, tiled=True)]
    psum x1 -> x0, waiting for transfers between devices: 115 us -> none  [spread(): return lax.psum(jnp.where(mine, value, jnp.zeros_like(value)), axis)]
    pallas_call x0 -> x1, Pallas kernels: none -> 67.7 us  [shards(): pl.pallas_call(kernel, out_shape=(jax.ShapeDtypeStruct((ROWS, WINDOW), BF...]
    select_n x291 -> x0, other arithmetic: 34 us -> none  [the longest x256 28.9 us: sweep_step(): panel_cols = jnp.where(select, pruned_col[:, None], panel_cols)]
    dynamic_slice x32 -> x0, local copies, waits for them, and re-layouts: 22.1 us -> none  [sweep_step(): pivot_value = lax.dynamic_slice_in_dim(chol_row, column_at, 1, 0)[0]]
    dot_general x9 -> x0, matrix products: 18.5 us -> none  [the longest x7 8.21 us: sweep_panel(): jnp.dot(block_errors, head_block[start:stop, stop:], precision=lax.Precis...]
  transfers between devices with their start and end apart: 3 -> 0, of which waited for: 3 -> 0; matrix products, arithmetic and copies ran while one was open for 0% -> 0% of each run, Pallas kernels for 0% -> 0%
where the time goes in v1:
time: 75 us; the launch traced here: 74.7 us
  Pallas kernels  67.7 us (90%)
  local copies, waits for them, and re-layouts  6.34 us (8%)
    pallas_call x1, Pallas kernels, shards(): pl.pallas_call(kernel, out_shape=(jax.ShapeDtypeStruct((ROWS, WINDOW), BF...  67.7 us
    unnamed x8, local copies, waits for them, and re-layouts  6.34 us

profile of v1, /device:TPU:1, one launch (start us, length us, event | category | flops | bytes accessed | tf_op | source)
XLA Modules:
  0.0 74.7 jit_solution(1586240586856384260)
XLA Ops:
  0.6 0.8 %copy.7.pattern = s32[104,64]{1,0:T(8,128)S(1)} copy(s32[104,64]{0,1:T(8,128)} %param.7) | data formatting | bytes 53248 | tf_op args[3]
  1.5 0.9 %copy.6.inverse = f32[256,64]{1,0:T(8,128)S(1)} copy(f32[256,64]{0,1:T(8,128)} %param.6) | data formatting | bytes 131072 | tf_op args[2]
  2.4 0.0 copy-start
  2.4 1.9 %copy-done = bf16[768,2048]{1,0:T(8,128)(2,1)S(1)} copy-done((bf16[768,2048]{1,0:T(8,128)(2,1)S(1)}, bf16[768,2048]{1,0:T(8,128)(2,1)}, u32[]{:S(2)}) %copy-start) | copy-done | bytes 3145752
  4.3 0.0 copy-start.1
  4.3 1.2 %copy-done.1 = bf16[104,4096]{1,0:T(8,128)(2,1)S(1)} copy-done((bf16[104,4096]{1,0:T(8,128)(2,1)S(1)}, bf16[104,4096]{1,0:T(8,128)(2,1)}, u32[]{:S(2)}) %copy-start.1) | copy-done | bytes 851992
  5.5 67.7 %shard_map.59 = (bf16[104,4096]{1,0:T(8,128)(2,1)S(1)}, f32[4,2048]{1,0:T(4,128)S(1)}) custom-call(bf16[768,2048]{1,0:T(8,128)(2,1)S(1)} %copy-done, bf16[104,4096]{1,0:T(8,128)(2,1)S(1)} %copy-done.1, f32[256,64]{1,0:T(8,128)S(1)} %copy.6.inverse, s32[104,64]{1,0:T(8,128)S(1)} %copy.7.pattern), custom_call_target="tpu_custom_call" | custom-call | flops 2000000000 | bytes 8000000 | tf_op jit(solution)/shard_map/pallas_call | solution.py:445
  73.1 0.9 %copy.10 = bf16[104,4096]{1,0:T(8,128)(2,1)} copy(bf16[104,4096]{1,0:T(8,128)(2,1)S(1)} %get-tuple-element.4) | data formatting | bytes 1703936
  74.0 0.6 copy.11
Async XLA Ops:
  2.4 1.9 %copy-start = (bf16[768,2048]{1,0:T(8,128)(2,1)S(1)}, bf16[768,2048]{1,0:T(8,128)(2,1)}, u32[]{:S(2)}) copy-start(bf16[768,2048]{1,0:T(8,128)(2,1)} %calib.1) | copy-start | bytes 9437188
  4.3 1.2 %copy-start.1 = (bf16[104,4096]{1,0:T(8,128)(2,1)S(1)}, bf16[104,4096]{1,0:T(8,128)(2,1)}, u32[]{:S(2)}) copy-start(bf16[104,4096]{1,0:T(8,128)(2,1)} %weights.1) | copy-start | bytes 2555908

commit v2 on v1

v2 whole, which is shorter than its diff:
```python
import jax
import jax.numpy as jnp
from jax import lax
from jax.experimental import pallas as pl
from jax.experimental.pallas import tpu as pltpu
from jax.sharding import PartitionSpec as P

MESH = pl.DeviceIdType.MESH
NZ, NY, NC, NH, NX = 8, 4, 2, 2, 4
PANEL_W = 256
WINDOW = 4096
ROWS = 104
LANES = 128
FEAT = 2048
TOK = 768
QTOK = TOK // NX
PART = PANEL_W // (NX * NC)
OWNER_X, OWNER_H = 2, 1
BLOCK = 32
CODE_MAX = 32767.0
CHOL_MAX = 2.0
SUM_MAX = 32000.0
F32 = jnp.float32
BF16 = jnp.bfloat16
HIGHEST = lax.Precision.HIGHEST


def contract(a, b, da, db, precision=None):
    return lax.dot_general(
        a, b, (((da,), (db,)), ((), ())), precision=precision, preferred_element_type=F32
    )


def identity(n, dtype):
    rows = lax.broadcasted_iota(jnp.int32, (n, n), 0)
    cols = lax.broadcasted_iota(jnp.int32, (n, n), 1)
    return jnp.where(rows == cols, 1.0, 0.0).astype(dtype)


def panel_order():
    rows = lax.broadcasted_iota(jnp.int32, (PANEL_W, PANEL_W), 0)
    cols = lax.broadcasted_iota(jnp.int32, (PANEL_W, PANEL_W), 1)
    core, rest = rows // 128, rows % 128
    feature = (rest // 4) * 8 + core * 4 + rest % 4
    return jnp.where(feature == cols, 1.0, 0.0).astype(BF16)


def encode_chol(value):
    root = jnp.sqrt(jnp.minimum(jnp.abs(value) * (1.0 / CHOL_MAX), 1.0)) * CODE_MAX
    code = jnp.round(jnp.where(value < 0.0, -root, root))
    return code.astype(jnp.int32).astype(jnp.int16)


def decode_chol(code):
    value = code.astype(jnp.int32).astype(F32)
    return value * jnp.abs(value) * (CHOL_MAX / (CODE_MAX * CODE_MAX))


ORDER = (0, 1, 7, 2, 6, 3, 5, 4)


def kernel(
    calib, weights, inverse, pattern,
    pruned, gram,
    xv, pv, wv, kv, iv, ipeer, blk, qv, hv, gv, msend, mrecv, ysend, yrecv,
    wpad, kpad, dg, ct, av, et, eh, el, po, pt,
    lsem, isem, s1s, s1r, hcs, hcr, s2s, s2r,
    qys, qyr, qzs, qzr, qxs, qxr, qcs, qcr, hys, hyr, hzs, hzr, hxs, hxr, hs, hr,
    xcs, xcr, rzs, rzr, rys, ryr,
):
    d = lax.axis_index("dp")
    t = lax.axis_index("tensor")
    z, y, c = d // (NY * NC), (d // NC) % NY, d % NC
    h, x = t // NX, t % NX
    owner = (h == OWNER_H) & (x == OWNER_X)
    not_owner = jnp.logical_not(owner)
    owner_side = h == OWNER_H

    def at(z=z, y=y, c=c, h=h, x=x):
        return ((z * NY + y) * NC + c, h * NX + x)

    def remote(src, dst, send, recv, where):
        return pltpu.make_async_remote_copy(
            src_ref=src, dst_ref=dst, send_sem=send, recv_sem=recv,
            device_id=where, device_id_type=MESH,
        )

    def zp(k):
        return lax.rem(z + k + NZ, NZ)

    def yp(k):
        return lax.rem(y + k, NY)

    def xp(k):
        return lax.rem(x + k, NX)

    def span(start, size):
        return pl.ds(pl.multiple_of(start, size), size)

    load_i = pltpu.make_async_copy(inverse, iv, lsem.at[0])
    load_x = pltpu.make_async_copy(calib, xv.at[c], lsem.at[1])
    load_w = pltpu.make_async_copy(weights, wv, lsem.at[2])
    load_k = pltpu.make_async_copy(pattern, kv, lsem.at[3])
    load_p = pltpu.make_async_copy(calib.at[:, pl.ds(0, PANEL_W)], pv, lsem.at[4])
    pl.when(owner)(load_p.start)
    load_i.start()
    load_x.start()
    load_w.start()
    load_k.start()

    barrier = pltpu.get_barrier_semaphore()
    partners = [at(c=1 - c), at(h=1 - h), at(h=1 - h, c=1 - c)]
    partners += [at(x=xp(k), c=1 - c) for k in range(1, NX)]
    partners += [at(z=zp(k)) for k in range(1, NZ)]
    partners += [at(y=yp(k)) for k in range(1, NY)]
    partners += [at(x=xp(k)) for k in range(1, NX)]
    for partner in partners:
        pl.semaphore_signal(barrier, inc=1, device_id=partner, device_id_type=MESH)

    @pl.when(owner)
    def _():
        load_p.wait()
        po[...] = contract(panel_order(), pv[...], 1, 1).astype(BF16)
        pt[c] = po[span(c * 128, 128), :]

    load_i.wait()
    pl.semaphore_wait(barrier, len(partners))

    def ordered(a, xo):
        return po.at[span(a * 128 + xo * PART, PART)]

    def piece(s, xo):
        return pt.at[s, span(xo * PART, PART)]

    def scatter(a, k):
        return remote(ordered(a, xp(k)), piece(c, xp(k)), s1s.at[a * 3 + k - 1], s1r.at[c], at(x=xp(k), c=a))

    def scattered(s):
        return remote(piece(s, x), piece(s, x), s1s.at[s], s1r.at[s], at(x=xp(1)))

    def across_owner(a):
        return remote(ordered(a, x), piece(c, x), hcs.at[a], hcr.at[c], at(h=1 - h, c=a))

    def across(s):
        return remote(piece(s, x), piece(s, x), hcs.at[s], hcr.at[s], at(h=1 - h))

    def share_owner(a, k):
        sem = s2r.at[c * 3 + k - 1]
        return remote(ordered(a, x), piece(c, x), s2s.at[a * 3 + k - 1], sem, at(x=xp(k), c=a))

    def share(s, k):
        return remote(piece(s, x), piece(s, x), s2s.at[s * 3 + k - 1], s2r.at[s * 3 + k - 1], at(x=xp(k)))

    def shared(s, k):
        src = piece(s, xp(NX - k))
        return remote(src, src, s2s.at[s * 3 + k - 1], s2r.at[s * 3 + k - 1], at(x=xp(k)))

    swap_p = remote(po.at[span((1 - c) * 128, 128)], pt.at[c], xcs.at[0], xcr.at[0], at(c=1 - c))
    swap_x = remote(xv.at[c], xv.at[c], xcs.at[1], xcr.at[1], at(c=1 - c))

    def to_owner(k):
        return owner_side & (xp(k) == OWNER_X)

    def start_share(a):
        for k in (2, 1, 3):
            pl.when(jnp.logical_not(to_owner(k)))(share(a, k).start)

    pair = remote(iv, ipeer, isem.at[0], isem.at[1], at(c=1 - c))
    pair.start()

    @pl.when(owner)
    def _():
        for a in range(2):
            for k in (2, 1, 3):
                scatter(a, k).start()
            across_owner(a).start()
        swap_p.start()

    load_x.wait()
    swap_x.start()

    part = span(c * 128 + x * PART, PART)
    half = span(c * 128, 128)
    other = span((1 - c) * 128, 128)
    head_chip = (z == 0) & (y < 2)
    hcols = span(jnp.minimum(y, 1) * 128, 128)

    pair.wait_recv()
    even = jnp.full(iv.shape, c, jnp.int32) == 0
    blk[...] = jnp.concatenate(
        [jnp.where(even, iv[...], ipeer[...]), jnp.where(even, ipeer[...], iv[...])], axis=0
    ).T

    @pl.when(head_chip)
    def _():
        hv[part, hcols] = blk[part, :]

    h_y = [
        remote(hv.at[part, hcols], hv.at[part, hcols], hys.at[k - 1], hyr.at[k - 1], at(y=yp(k)))
        for k in range(1, NY)
    ]

    @pl.when(head_chip)
    def _():
        for copy in h_y:
            copy.start()

    qv[z, part, span(y * 128, 128)] = encode_chol(blk[part, :])
    mine = qv.at[z, part, span(y * 128, 128)]
    q_y = [remote(mine, mine, qys.at[k - 1], qyr.at[k - 1], at(y=yp(k))) for k in range(1, NY)]
    for copy in q_y:
        copy.start()

    @pl.when(owner_side & not_owner)
    def _():
        for s in range(2):
            scattered(s).wait_recv()
            across(s).start()
        for s in range(2):
            start_share(s)

    @pl.when(owner)
    def _():
        for a in range(2):
            for k in range(1, NX):
                scatter(a, k).wait_send()
        for a in range(2):
            for k in (2, 1, 3):
                share_owner(a, k).start()

    @pl.when(z == 0)
    def _():
        for k in range(1, NY):
            yo = yp(NY - k)
            cols = span(jnp.minimum(yo, 1) * 128, 128)

            @pl.when(yo < 2)
            def _():
                remote(hv.at[part, cols], hv.at[part, cols], hys.at[k - 1], hyr.at[k - 1], at(y=yp(k))).wait_recv()

    h_z = [remote(hv.at[part], hv.at[part], hzs.at[k - 1], hzr.at[0], at(z=zp(k))) for k in range(1, NZ)]

    @pl.when(z == 0)
    def _():
        for k in (4, 3, 5, 2, 6, 1, 7):
            h_z[k - 1].start()

    for k in range(1, NY):
        src = qv.at[z, part, span(yp(NY - k) * 128, 128)]
        remote(src, src, qys.at[k - 1], qyr.at[k - 1], at(y=yp(k))).wait_recv()

    def over_z(k):
        return remote(qv.at[z, part], qv.at[z, part], qzs.at[k - 1], qzr.at[k - 1], at(z=zp(k)))

    def came_over_z(k):
        src = qv.at[zp(NZ - k), part]
        return remote(src, src, qzs.at[k - 1], qzr.at[k - 1], at(z=zp(k)))

    def over_x(j, k):
        src = qv.at[zp(ORDER[j]), part]
        return remote(src, src, qxs.at[j * 3 + k - 1], qxr.at[j * 3 + k - 1], at(x=xp(k)))

    def start_over_x(j):
        if j:
            came_over_z(NZ - ORDER[j]).wait_recv()
        for k in (2, 1, 3):
            over_x(j, k).start()

    for k in (1, 7, 2, 6, 3, 5, 4):
        over_z(k).start()

    load_w.wait()
    load_k.wait()
    wpad[...] = jnp.zeros_like(wpad)
    wpad[0:ROWS, :] = wv[:, 0:PANEL_W].astype(F32)
    kpad[...] = jnp.zeros_like(kpad)
    kpad[0:64, 0:ROWS] = kv[...].astype(F32)
    ct[...] = contract(identity(PANEL_W, BF16), wpad[...].astype(BF16), 1, 1)
    col_id = lax.broadcasted_iota(jnp.int32, (PANEL_W, LANES), 0)
    group_id = lax.broadcasted_iota(jnp.int32, (PANEL_W, LANES), 1)
    repeat = jnp.where(col_id // 4 == group_id, 1.0, 0.0).astype(BF16)
    choice = contract(repeat, kpad[...].astype(BF16), 1, 0).astype(jnp.int32)
    place = col_id % 4
    drop = (
        ((place == 0) & (choice >= 3))
        | ((place == 1) & ((choice == 1) | (choice == 2) | (choice == 5)))
        | ((place == 2) & ((choice == 0) | (choice == 2) | (choice == 4)))
        | ((place == 3) & ((choice == 0) | (choice == 1) | (choice == 3)))
    )
    av[...] = jnp.where(drop, 1.0, 0.0)

    @pl.when(jnp.logical_not(owner_side))
    def _():
        for s in range(2):
            across(s).wait_recv()
            start_share(s)

    @pl.when(z > 0)
    def _():
        h_z[0].wait_recv()

    h_x = [remote(hv.at[part], hv.at[part], hxs.at[k - 1], hxr.at[k - 1], at(x=xp(k))) for k in range(1, NX)]
    for copy in h_x:
        copy.start()

    def gram_part(s):
        @pl.when(not_owner)
        def _():
            for k in range(1, NX):
                shared(s, k).wait_recv()

        for tile in range(4):
            cols = slice(tile * 512, tile * 512 + 512)
            value = contract(pt[s], xv[s, :, cols], 1, 0)
            gv[tile] = value if s == 0 else gv[tile] + value

    @pl.when(owner)
    def _():
        swap_p.wait_recv()

    remote(xv.at[1 - c], xv.at[1 - c], xcs.at[1], xcr.at[1], at(c=1 - c)).wait_recv()
    gram_part(0)
    gram_part(1)

    def own_rows(zd):
        rows = span(zd * 16, 16)
        parts = [gv[tile, rows, :] for tile in range(4)]
        return [p[:, 128 * i : 128 * i + 128] for p in parts for i in range(4)]

    def place_of(tile):
        return tile if tile < 8 else tile + 1

    def pack(tiles, slot):
        most = jnp.abs(tiles[0])
        for value in tiles[1:]:
            most = jnp.maximum(most, jnp.abs(value))
        most = jnp.max(most, axis=0, keepdims=True)
        power = jnp.ceil(jnp.log2(jnp.maximum(most, 1e-30)))
        up = jnp.exp2(-power) * SUM_MAX
        for i, value in enumerate(tiles):
            msend[slot, place_of(i)] = jnp.round(value * up).astype(jnp.int32).astype(jnp.int16)
        msend[slot, 8] = jnp.broadcast_to(power, (16, 128)).astype(jnp.int32).astype(jnp.int16)

    def add(tiles, slot, low=0, high=16):
        down = jnp.exp2(mrecv[slot, 8].astype(jnp.int32).astype(F32)) * (1.0 / SUM_MAX)
        return [
            value + mrecv[slot, place_of(i)].astype(jnp.int32).astype(F32) * down if low <= i < high else value
            for i, value in enumerate(tiles)
        ]

    def message(slot_from, slot_to, k, which=None):
        src, dst = msend.at[slot_from], mrecv.at[slot_to]
        if which is not None:
            src, dst = src.at[pl.ds(8 * which, 9)], dst.at[pl.ds(8 * which, 9)]
        return remote(src, dst, rzs.at[slot_to], rzr.at[slot_to], at(z=zp(k)))

    far = [message(0, 0, 1), message(1, 1, -1), message(2, 2, 2, 0), message(2, 3, -2, 1)]
    near = [message(3, 4, 1), message(4, 5, -1)]
    second = [message(5, 6, 2), message(6, 7, -2)]
    pack(own_rows(zp(4)), 2)
    far[2].start()
    far[3].start()
    pack(own_rows(zp(3)), 0)
    far[0].start()
    pack(own_rows(zp(-3)), 1)
    far[1].start()
    for j in range(3):
        start_over_x(j)
    pack(own_rows(zp(1)), 3)
    near[0].start()
    pack(own_rows(zp(-1)), 4)
    near[1].start()

    for k in range(1, NX):
        rows = span(c * 128 + xp(NX - k) * PART, PART)
        remote(hv.at[rows], hv.at[rows], hxs.at[k - 1], hxr.at[k - 1], at(x=xp(k))).wait_recv()
    h_c = remote(hv.at[half], hv.at[half], hs.at[0], hr.at[0], at(c=1 - c))
    h_c.start()

    for j in range(3, NZ):
        start_over_x(j)

    remote(hv.at[other], hv.at[other], hs.at[0], hr.at[0], at(c=1 - c)).wait_recv()
    head = hv[...]
    row_id = lax.broadcasted_iota(jnp.int32, (PANEL_W, PANEL_W), 0)
    lane_id = lax.broadcasted_iota(jnp.int32, (PANEL_W, PANEL_W), 1)
    pivot = jnp.sum(jnp.where(row_id == lane_id, head, 0.0), axis=1, keepdims=True)
    av[...] = av[...] * (1.0 / pivot)
    upper = jnp.where(lane_id > row_id, head, 0.0).T
    for b in range(PANEL_W // BLOCK):
        at_b = b * BLOCK
        dg[b, :, 0:BLOCK] = upper[at_b : at_b + BLOCK, at_b : at_b + BLOCK]

    def sweep(b, carry):
        rows = span(b * BLOCK, BLOCK)
        factor = av[rows, :]
        corner = dg[b]
        now = ct[rows, :]
        cols = [now[8 * v : 8 * v + 8, :] for v in range(BLOCK // 8)]
        for j in range(BLOCK):
            v0 = j // 8
            err = cols[v0][j % 8 : j % 8 + 1, :] * factor[j : j + 1, :]
            for v in range(v0, BLOCK // 8):
                cols[v] = cols[v] - corner[8 * v : 8 * v + 8, j : j + 1] * err
        done = jnp.concatenate(cols, axis=0)
        errors = done * factor
        et[rows, :] = errors
        update = contract(hv[rows, :], errors, 0, 0, HIGHEST)
        later = col_id >= (b + 1) * BLOCK
        ct[...] = ct[...] - jnp.where(later, update, 0.0)
        ct[rows, :] = done
        return carry

    lax.fori_loop(0, 4, sweep, 0)

    for copy in far:
        copy.wait_recv()
    pack(add(add(own_rows(zp(2)), 0), 2, 0, 8), 5)
    second[0].start()
    pack(add(add(own_rows(zp(-2)), 1), 3, 8, 16), 6)
    second[1].start()

    lax.fori_loop(4, PANEL_W // BLOCK, sweep, 0)
    kept = jnp.where(drop, 0.0, ct[...]).astype(BF16)
    eye = identity(PANEL_W, BF16)
    kept_rows = contract(kept, eye, 0, 0)
    errors = et[...]
    errors_hi = errors.astype(BF16)
    errors_lo = (errors - errors_hi.astype(F32)).astype(BF16)
    eh[...] = contract(errors_hi, eye, 0, 0).astype(BF16)
    el[...] = contract(errors_lo, eye, 0, 0).astype(BF16)

    def block_z(j):
        rel = jnp.where(j % 2 == 1, (j + 1) // 2, (NZ - j // 2) % NZ)
        return lax.rem(z + rel, NZ)

    def between(j, rows):
        src = qv.at[block_z(j), rows]
        return remote(src, src, qcs.at[j], qcr.at[j], at(c=1 - c))

    def hand_over(j):
        for k in range(1, NX):
            src = qv.at[block_z(j), span(c * 128 + xp(NX - k) * PART, PART)]
            remote(src, src, qxs.at[j * 3 + k - 1], qxr.at[j * 3 + k - 1], at(x=xp(k))).wait_recv()
        between(j, half).start()

    for copy in near + second:
        copy.wait_recv()
    tiles = own_rows(z)
    for slot in range(4, 8):
        tiles = add(tiles, slot)
    for tile in range(4):
        summed = jnp.concatenate(tiles[4 * tile : 4 * tile + 4], axis=1)
        for yd in range(NY):
            ysend[yd, tile * 4 : tile * 4 + 4, :] = summed[yd * 4 : yd * 4 + 4, :]
    r_y = [
        remote(ysend.at[yp(k)], yrecv.at[k - 1], rys.at[k - 1], ryr.at[k - 1], at(y=yp(k)))
        for k in range(1, NY)
    ]
    for copy in r_y:
        copy.start()

    hand_over(0)
    hand_over(1)
    hand_over(2)

    def tail(j, carry):
        @pl.when(j + 3 < NZ)
        def _():
            hand_over(j + 3)

        between(j, other).wait_recv()
        zb = block_z(j)
        for i in range(2):
            chol = decode_chol(qv[zb, :, 256 * i : 256 * i + 256])
            chol_hi = chol.astype(BF16)
            chol_lo = (chol - chol_hi.astype(F32)).astype(BF16)
            update = contract(eh[...], chol_hi, 1, 0) + (
                contract(eh[...], chol_lo, 1, 0) + contract(el[...], chol_hi, 1, 0)
            )
            cols = span(zb * 512 + i * 256, 256)
            pruned[:, cols] = (wv[:, cols].astype(F32) - update[0:ROWS, :]).astype(BF16)
        return carry

    lax.fori_loop(0, NZ, tail, 0)
    pruned[:, 0:PANEL_W] = kept_rows[0:ROWS, :].astype(BF16)

    for copy in r_y:
        copy.wait_recv()
    total = ysend[y] + yrecv[0] + yrecv[1] + yrecv[2]
    total = total * (2.0 / (TOK * NZ * NY * NC))
    for tile in range(4):
        gram[:, tile * 512 : tile * 512 + 512] = total[tile * 4 : tile * 4 + 4, :]

    @pl.when(owner)
    def _():
        swap_p.wait_send()
        for a in range(2):
            across_owner(a).wait_send()
            for k in range(1, NX):
                share_owner(a, k).wait_send()

    for s in range(2):
        pl.when(owner_side & not_owner)(across(s).wait_send)
        for k in range(1, NX):
            pl.when(not_owner & jnp.logical_not(to_owner(k)))(share(s, k).wait_send)

    @pl.when(head_chip)
    def _():
        for copy in h_y:
            copy.wait_send()

    @pl.when(z == 0)
    def _():
        for copy in h_z:
            copy.wait_send()

    for copy in [pair, h_c, swap_x] + q_y + h_x + far + near + second + r_y:
        copy.wait_send()
    for k in range(1, NZ):
        over_z(k).wait_send()
    for j in range(NZ):
        for k in range(1, NX):
            over_x(j, k).wait_send()
        between(j, half).wait_send()


def shards(calib_inputs, weights, inverse_chol, keep_pattern):
    dma = pltpu.SemaphoreType.DMA
    vmem = pltpu.VMEM
    scratch = [
        vmem((NC, TOK, FEAT), BF16),
        vmem((TOK, PANEL_W), BF16),
        vmem((ROWS, WINDOW), BF16),
        vmem((64, ROWS), jnp.int32),
        vmem((64, PANEL_W), F32),
        vmem((64, PANEL_W), F32),
        vmem((PANEL_W, 128), F32),
        vmem((NZ, PANEL_W, NY * 128), jnp.int16),
        vmem((PANEL_W, PANEL_W), F32),
        vmem((4, 128, 512), F32),
        vmem((7, 17, 16, 128), jnp.int16),
        vmem((8, 17, 16, 128), jnp.int16),
        vmem((NY, 16, 512), F32),
        vmem((NY - 1, 16, 512), F32),
        vmem((LANES, PANEL_W), F32),
        vmem((LANES, LANES), F32),
        vmem((PANEL_W // BLOCK, BLOCK, 128), F32),
        vmem((PANEL_W, LANES), F32),
        vmem((PANEL_W, LANES), F32),
        vmem((PANEL_W, LANES), F32),
        vmem((LANES, PANEL_W), BF16),
        vmem((LANES, PANEL_W), BF16),
        vmem((PANEL_W, TOK), BF16),
        vmem((NC, 128, TOK), BF16),
    ]
    sems = [5, 2, 6, 2, 2, 2, 6, 6, 3, 3, 7, 7, 24, 24, 8, 8, 3, 3, 7, 1, 3, 3, 1, 1, 2, 2, 8, 8, 3, 3]
    scratch += [dma((n,)) for n in sems]
    anywhere = pl.BlockSpec(memory_space=pltpu.HBM)
    inside = pl.BlockSpec(memory_space=pltpu.VMEM)
    return pl.pallas_call(
        kernel,
        out_shape=(
            pltpu.VMEM((ROWS, WINDOW), BF16),
            pltpu.VMEM((PANEL_W // (NZ * NY * NC), FEAT), F32),
        ),
        in_specs=[anywhere] * 4,
        out_specs=(inside, inside),
        scratch_shapes=scratch,
        compiler_params=pltpu.CompilerParams(
            collective_id=0, has_side_effects=True, vmem_limit_bytes=40 * 2**20
        ),
        cost_estimate=pl.CostEstimate(flops=2 * 10**9, bytes_accessed=8 * 10**6, transcendentals=0),
    )(*[pltpu.with_memory_space_constraint(v, pltpu.HBM) for v in (calib_inputs, weights, inverse_chol.T, keep_pattern.T)])


def solution(mesh):
    placed = (
        P("dp", "tensor"),
        P(("dp", "tensor"), None),
        P(None, "dp"),
        P(("dp", "tensor"), None),
    )
    return jax.shard_map(
        shards,
        mesh=mesh,
        in_specs=placed,
        out_specs=(P(("dp", "tensor"), None), P("dp", "tensor")),
        check_vma=False,
    )
```

time: 75 us -> 52.4 us (0.70)
  Pallas kernels: 67.7 us -> 49.3 us
  local copies, waits for them, and re-layouts: 6.34 us -> 1.52 us
    pallas_call x1, Pallas kernels: 67.7 us -> 49.3 us  [shards(): pl.pallas_call(kernel, out_shape=(pltpu.VMEM((ROWS, WINDOW), BF16), pltpu...]
    unnamed x8 -> x2, local copies, waits for them, and re-layouts: 6.34 us -> 1.52 us
where the time goes in v2:
time: 52.4 us; the launch traced here: 51.4 us
  Pallas kernels  49.3 us (94%)
  local copies, waits for them, and re-layouts  1.52 us (3%)
  between operations  0.64 us (1%)
    pallas_call x1, Pallas kernels, shards(): pl.pallas_call(kernel, out_shape=(pltpu.VMEM((ROWS, WINDOW), BF16), pltpu...  49.3 us
    unnamed x2, local copies, waits for them, and re-layouts  1.52 us

profile of v2, /device:TPU:1, one launch (start us, length us, event | category | flops | bytes accessed | tf_op | source)
XLA Modules:
  0.0 51.4 jit_solution(10748644500423046080)
XLA Ops:
  0.6 49.3 %shard_map.59 = (bf16[104,4096]{1,0:T(8,128)(2,1)S(1)}, f32[4,2048]{1,0:T(4,128)S(1)}) custom-call(bf16[768,2048]{1,0:T(8,128)(2,1)} %calib.1, bf16[104,4096]{1,0:T(8,128)(2,1)} %weights.1, f32[64,256]{1,0:T(8,128)} %bitcast.2, s32[64,104]{1,0:T(8,128)} %bitcast.3), custom_call_target="tpu_custom_call" | custom-call | flops 2000000000 | bytes 8000000 | tf_op jit(solution)/shard_map/pallas_call | solution.py:561
  49.9 0.9 %copy.8 = bf16[104,4096]{1,0:T(8,128)(2,1)} copy(bf16[104,4096]{1,0:T(8,128)(2,1)S(1)} %get-tuple-element.2) | data formatting | bytes 1703936
  50.8 0.6 %copy.9 = f32[4,2048]{1,0:T(4,128)} copy(f32[4,2048]{1,0:T(4,128)S(1)} %get-tuple-element.3) | data formatting | bytes 65536

commit v3 on v2

--- a/solution.py
+++ b/solution.py
@@ -15,6 +15,7 @@
 TOK = 768
 QTOK = TOK // NX
 PART = PANEL_W // (NX * NC)
+SHARE = PANEL_W // (2 * NC)
 OWNER_X, OWNER_H = 2, 1
 BLOCK = 32
 CODE_MAX = 32767.0
@@ -57,6 +58,7 @@
 
 
 ORDER = (0, 1, 7, 2, 6, 3, 5, 4)
+GROUPS = ((0, 1), (1, 2), (2, 3), (3, 4), (4, 5), (5, 6), (6, 7), (7, 8))
 
 
 def kernel(
@@ -109,11 +111,10 @@
     load_k.start()
 
     barrier = pltpu.get_barrier_semaphore()
-    partners = [at(c=1 - c), at(h=1 - h), at(h=1 - h, c=1 - c)]
-    partners += [at(x=xp(k), c=1 - c) for k in range(1, NX)]
+    partners = [at(x=xp(k), c=c) for k in range(1, NX)] + [at(x=xp(k), c=1 - c) for k in range(1, NX)]
+    partners += [at(h=1 - h), at(h=1 - h, c=1 - c), at(c=1 - c)]
+    partners += [at(y=yp(k)) for k in range(1, NY)]
     partners += [at(z=zp(k)) for k in range(1, NZ)]
-    partners += [at(y=yp(k)) for k in range(1, NY)]
-    partners += [at(x=xp(k)) for k in range(1, NX)]
     for partner in partners:
         pl.semaphore_signal(barrier, inc=1, device_id=partner, device_id_type=MESH)
 
@@ -138,22 +139,30 @@
     def scattered(s):
         return remote(piece(s, x), piece(s, x), s1s.at[s], s1r.at[s], at(x=xp(1)))
 
-    def across_owner(a):
-        return remote(ordered(a, x), piece(c, x), hcs.at[a], hcr.at[c], at(h=1 - h, c=a))
-
-    def across(s):
-        return remote(piece(s, x), piece(s, x), hcs.at[s], hcr.at[s], at(h=1 - h))
-
-    def share_owner(a, k):
-        sem = s2r.at[c * 3 + k - 1]
-        return remote(ordered(a, x), piece(c, x), s2s.at[a * 3 + k - 1], sem, at(x=xp(k), c=a))
-
-    def share(s, k):
-        return remote(piece(s, x), piece(s, x), s2s.at[s * 3 + k - 1], s2r.at[s * 3 + k - 1], at(x=xp(k)))
-
-    def shared(s, k):
-        src = piece(s, xp(NX - k))
-        return remote(src, src, s2s.at[s * 3 + k - 1], s2r.at[s * 3 + k - 1], at(x=xp(k)))
+    def across_owner(a, u):
+        src = po.at[span(a * 128 + x * PART + u * 16, 16)]
+        return remote(src, sub(c, x, u), hcs.at[a * 2 + u], hcr.at[c * 2 + u], at(h=1 - h, c=a))
+
+    def sub(s, xo, u):
+        return pt.at[s, span(xo * PART + u * 16, 16)]
+
+    def across(s, u):
+        sem = s * 2 + u
+        return remote(sub(s, x, u), sub(s, x, u), hcs.at[sem], hcr.at[sem], at(h=1 - h))
+
+    def share_owner(a, k, u):
+        src = po.at[span(a * 128 + x * PART + u * 16, 16)]
+        sem = s2r.at[(c * 3 + k - 1) * 2 + u]
+        return remote(src, sub(c, x, u), s2s.at[(a * 3 + k - 1) * 2 + u], sem, at(x=xp(k), c=a))
+
+    def share(s, k, u):
+        sem = (s * 3 + k - 1) * 2 + u
+        return remote(sub(s, x, u), sub(s, x, u), s2s.at[sem], s2r.at[sem], at(x=xp(k)))
+
+    def shared(s, k, u):
+        src = sub(s, xp(NX - k), u)
+        sem = (s * 3 + k - 1) * 2 + u
+        return remote(src, src, s2s.at[sem], s2r.at[sem], at(x=xp(k)))
 
     swap_p = remote(po.at[span((1 - c) * 128, 128)], pt.at[c], xcs.at[0], xcr.at[0], at(c=1 - c))
     swap_x = remote(xv.at[c], xv.at[c], xcs.at[1], xcr.at[1], at(c=1 - c))
@@ -161,9 +170,9 @@
     def to_owner(k):
         return owner_side & (xp(k) == OWNER_X)
 
-    def start_share(a):
+    def start_share(s, u):
         for k in (2, 1, 3):
-            pl.when(jnp.logical_not(to_owner(k)))(share(a, k).start)
+            pl.when(jnp.logical_not(to_owner(k)))(share(s, k, u).start)
 
     pair = remote(iv, ipeer, isem.at[0], isem.at[1], at(c=1 - c))
     pair.start()
@@ -173,13 +182,25 @@
         for a in range(2):
             for k in (2, 1, 3):
                 scatter(a, k).start()
-            across_owner(a).start()
+            for u in range(2):
+                across_owner(a, u).start()
         swap_p.start()
 
     load_x.wait()
     swap_x.start()
 
-    part = span(c * 128 + x * PART, PART)
+    part = span(c * 128 + (x % 2) * SHARE, SHARE)
+
+    def lower(parity):
+        return span(c * 128 + parity * SHARE, SHARE // 2)
+
+    def upper_of(parity):
+        return span(c * 128 + parity * SHARE + SHARE // 2, SHARE // 2)
+
+    even_x = x % 2
+    lends = (lower(even_x), upper_of(even_x))
+    lacks = (lower(1 - even_x), upper_of(1 - even_x))
+    sides = (xp(1), xp(3))
     half = span(c * 128, 128)
     other = span((1 - c) * 128, 128)
     head_chip = (z == 0) & (y < 2)
@@ -205,8 +226,8 @@
         for copy in h_y:
             copy.start()
 
-    qv[z, part, span(y * 128, 128)] = encode_chol(blk[part, :])
-    mine = qv.at[z, part, span(y * 128, 128)]
+    qv[0, part, span(y * 128, 128)] = encode_chol(blk[part, :])
+    mine = qv.at[0, part, span(y * 128, 128)]
     q_y = [remote(mine, mine, qys.at[k - 1], qyr.at[k - 1], at(y=yp(k))) for k in range(1, NY)]
     for copy in q_y:
         copy.start()
@@ -215,9 +236,11 @@
     def _():
         for s in range(2):
             scattered(s).wait_recv()
-            across(s).start()
+            for u in range(2):
+                across(s, u).start()
         for s in range(2):
-            start_share(s)
+            for u in range(2):
+                start_share(s, u)
 
     @pl.when(owner)
     def _():
@@ -226,7 +249,8 @@
                 scatter(a, k).wait_send()
         for a in range(2):
             for k in (2, 1, 3):
-                share_owner(a, k).start()
+                for u in range(2):
+                    share_owner(a, k, u).start()
 
     @pl.when(z == 0)
     def _():
@@ -246,28 +270,55 @@
             h_z[k - 1].start()
 
     for k in range(1, NY):
-        src = qv.at[z, part, span(yp(NY - k) * 128, 128)]
+        src = qv.at[0, part, span(yp(NY - k) * 128, 128)]
         remote(src, src, qys.at[k - 1], qyr.at[k - 1], at(y=yp(k))).wait_recv()
 
-    def over_z(k):
-        return remote(qv.at[z, part], qv.at[z, part], qzs.at[k - 1], qzr.at[k - 1], at(z=zp(k)))
-
-    def came_over_z(k):
-        src = qv.at[zp(NZ - k), part]
-        return remote(src, src, qzs.at[k - 1], qzr.at[k - 1], at(z=zp(k)))
-
-    def over_x(j, k):
-        src = qv.at[zp(ORDER[j]), part]
-        return remote(src, src, qxs.at[j * 3 + k - 1], qxr.at[j * 3 + k - 1], at(x=xp(k)))
-
-    def start_over_x(j):
-        if j:
-            came_over_z(NZ - ORDER[j]).wait_recv()
-        for k in (2, 1, 3):
-            over_x(j, k).start()
-
-    for k in (1, 7, 2, 6, 3, 5, 4):
-        over_z(k).start()
+    def block(rel, rows=part):
+        return qv.at[ORDER.index(rel % NZ), rows]
+
+    def over_z(n, k):
+        return remote(block(0), block(-k), qzs.at[n], qzr.at[n], at(z=zp(k)))
+
+    def came_over_z(n, k):
+        return remote(block(-k), block(-k), qzs.at[n], qzr.at[n], at(z=zp(k)))
+
+    def onward(n, k):
+        return remote(block(-2 * k), block(-3 * k), qzs.at[4 + n], qzr.at[4 + n], at(z=zp(k)))
+
+    def onward_half(n, k):
+        rows = span(c * 128 + even_x * SHARE + n * (SHARE // 2), SHARE // 2)
+        return remote(block(-2 * k, rows), block(4, rows), qzs.at[6 + n], qzr.at[6 + n], at(z=zp(2 * k)))
+
+    first_z = ((0, 2), (1, -2), (2, 1), (3, -1))
+
+    def came_onward(rel):
+        if rel == 4:
+            for n in range(2):
+                rows = span(c * 128 + even_x * SHARE + n * (SHARE // 2), SHARE // 2)
+                remote(block(4, rows), block(4, rows), qzs.at[6 + n], qzr.at[6 + n], at(z=zp(1))).wait_recv()
+        elif rel in (3, 5):
+            n = 1 if rel == 3 else 0
+            remote(block(rel), block(rel), qzs.at[4 + n], qzr.at[4 + n], at(z=zp(1))).wait_recv()
+        elif rel in (1, 7):
+            n = 2 if rel == 7 else 3
+            came_over_z(n, first_z[n][1]).wait_recv()
+
+    def group(g, rows):
+        low, high = GROUPS[g]
+        return qv.at[pl.ds(low, high - low), rows]
+
+    def over_x(g, n):
+        src = group(g, lends[n])
+        return remote(src, src, qxs.at[g * 2 + n], qxr.at[g * 2 + n], at(x=sides[n]))
+
+    def start_over_x(g):
+        for j in range(*GROUPS[g]):
+            came_onward(ORDER[j])
+        for n in range(2):
+            over_x(g, n).start()
+
+    for n, k in first_z:
+        over_z(n, k).start()
 
     load_w.wait()
     load_k.wait()
@@ -292,14 +343,20 @@
     @pl.when(jnp.logical_not(owner_side))
     def _():
         for s in range(2):
-            across(s).wait_recv()
-            start_share(s)
+            for u in range(2):
+                across(s, u).wait_recv()
+                start_share(s, u)
+
+    for n, k in ((0, 1), (1, -1)):
+        came_over_z(n, 2 * k).wait_recv()
+        onward(n, k).start()
+        onward_half(n, k).start()
 
     @pl.when(z > 0)
     def _():
         h_z[0].wait_recv()
 
-    h_x = [remote(hv.at[part], hv.at[part], hxs.at[k - 1], hxr.at[k - 1], at(x=xp(k))) for k in range(1, NX)]
+    h_x = [remote(hv.at[lends[n]], hv.at[lends[n]], hxs.at[n], hxr.at[n], at(x=sides[n])) for n in range(2)]
     for copy in h_x:
         copy.start()
 
@@ -307,7 +364,8 @@
         @pl.when(not_owner)
         def _():
             for k in range(1, NX):
-                shared(s, k).wait_recv()
+                for u in range(2):
+                    shared(s, k, u).wait_recv()
 
         for tile in range(4):
             cols = slice(tile * 512, tile * 512 + 512)
@@ -364,21 +422,19 @@
     far[0].start()
     pack(own_rows(zp(-3)), 1)
     far[1].start()
-    for j in range(3):
-        start_over_x(j)
     pack(own_rows(zp(1)), 3)
     near[0].start()
     pack(own_rows(zp(-1)), 4)
     near[1].start()
 
-    for k in range(1, NX):
-        rows = span(c * 128 + xp(NX - k) * PART, PART)
-        remote(hv.at[rows], hv.at[rows], hxs.at[k - 1], hxr.at[k - 1], at(x=xp(k))).wait_recv()
+    start_over_x(0)
+    for n in range(2):
+        remote(hv.at[lacks[n]], hv.at[lacks[n]], hxs.at[n], hxr.at[n], at(x=sides[n])).wait_recv()
     h_c = remote(hv.at[half], hv.at[half], hs.at[0], hr.at[0], at(c=1 - c))
     h_c.start()
 
-    for j in range(3, NZ):
-        start_over_x(j)
+    for g in range(1, len(GROUPS)):
+        start_over_x(g)
 
     remote(hv.at[other], hv.at[other], hs.at[0], hr.at[0], at(c=1 - c)).wait_recv()
     head = hv[...]
@@ -411,7 +467,8 @@
         ct[rows, :] = done
         return carry
 
-    lax.fori_loop(0, 4, sweep, 0)
+    lax.fori_loop(0, 2, sweep, 0)
+    lax.fori_loop(2, 4, sweep, 0)
 
     for copy in far:
         copy.wait_recv()
@@ -434,15 +491,18 @@
         rel = jnp.where(j % 2 == 1, (j + 1) // 2, (NZ - j // 2) % NZ)
         return lax.rem(z + rel, NZ)
 
-    def between(j, rows):
-        src = qv.at[block_z(j), rows]
-        return remote(src, src, qcs.at[j], qcr.at[j], at(c=1 - c))
-
-    def hand_over(j):
-        for k in range(1, NX):
-            src = qv.at[block_z(j), span(c * 128 + xp(NX - k) * PART, PART)]
-            remote(src, src, qxs.at[j * 3 + k - 1], qxr.at[j * 3 + k - 1], at(x=xp(k))).wait_recv()
-        between(j, half).start()
+    def between(g, rows):
+        src = group(g, rows)
+        return remote(src, src, qcs.at[g], qcr.at[g], at(c=1 - c))
+
+    def hand_over(g):
+        for n in range(2):
+            src = group(g, lacks[n])
+            remote(src, src, qxs.at[g * 2 + n], qxr.at[g * 2 + n], at(x=sides[n])).wait_recv()
+        between(g, half).start()
+
+    for g in range(8):
+        hand_over(g)
 
     for copy in near + second:
         copy.wait_recv()
@@ -460,19 +520,10 @@
     for copy in r_y:
         copy.start()
 
-    hand_over(0)
-    hand_over(1)
-    hand_over(2)
-
     def tail(j, carry):
-        @pl.when(j + 3 < NZ)
-        def _():
-            hand_over(j + 3)
-
-        between(j, other).wait_recv()
         zb = block_z(j)
         for i in range(2):
-            chol = decode_chol(qv[zb, :, 256 * i : 256 * i + 256])
+            chol = decode_chol(qv[j, :, 256 * i : 256 * i + 256])
             chol_hi = chol.astype(BF16)
             chol_lo = (chol - chol_hi.astype(F32)).astype(BF16)
             update = contract(eh[...], chol_hi, 1, 0) + (
@@ -482,7 +533,11 @@
             pruned[:, cols] = (wv[:, cols].astype(F32) - update[0:ROWS, :]).astype(BF16)
         return carry
 
-    lax.fori_loop(0, NZ, tail, 0)
+    for g, (low, high) in enumerate(GROUPS):
+        if g + 8 < len(GROUPS):
+            hand_over(g + 8)
+        between(g, other).wait_recv()
+        lax.fori_loop(low, high, tail, 0)
     pruned[:, 0:PANEL_W] = kept_rows[0:ROWS, :].astype(BF16)
 
     for copy in r_y:
@@ -496,14 +551,16 @@
     def _():
         swap_p.wait_send()
         for a in range(2):
-            across_owner(a).wait_send()
+            for u in range(2):
+                across_owner(a, u).wait_send()
+                for k in range(1, NX):
+                    share_owner(a, k, u).wait_send()
+
+    for s in range(2):
+        for u in range(2):
+            pl.when(owner_side & not_owner)(across(s, u).wait_send)
             for k in range(1, NX):
-                share_owner(a, k).wait_send()
-
-    for s in range(2):
-        pl.when(owner_side & not_owner)(across(s).wait_send)
-        for k in range(1, NX):
-            pl.when(not_owner & jnp.logical_not(to_owner(k)))(share(s, k).wait_send)
+                pl.when(not_owner & jnp.logical_not(to_owner(k)))(share(s, k, u).wait_send)
 
     @pl.when(head_chip)
     def _():
@@ -517,12 +574,15 @@
 
     for copy in [pair, h_c, swap_x] + q_y + h_x + far + near + second + r_y:
         copy.wait_send()
-    for k in range(1, NZ):
-        over_z(k).wait_send()
-    for j in range(NZ):
-        for k in range(1, NX):
-            over_x(j, k).wait_send()
-        between(j, half).wait_send()
+    for n, k in first_z:
+        over_z(n, k).wait_send()
+    for n, k in ((0, 1), (1, -1)):
+        onward(n, k).wait_send()
+        onward_half(n, k).wait_send()
+    for g in range(len(GROUPS)):
+        for n in range(2):
+            over_x(g, n).wait_send()
+        between(g, half).wait_send()
 
 
 def shards(calib_inputs, weights, inverse_chol, keep_pattern):
@@ -554,7 +614,7 @@
         vmem((PANEL_W, TOK), BF16),
         vmem((NC, 128, TOK), BF16),
     ]
-    sems = [5, 2, 6, 2, 2, 2, 6, 6, 3, 3, 7, 7, 24, 24, 8, 8, 3, 3, 7, 1, 3, 3, 1, 1, 2, 2, 8, 8, 3, 3]
+    sems = [5, 2, 6, 2, 4, 4, 12, 12, 3, 3, 8, 8, 16, 16, 8, 8, 3, 3, 7, 1, 3, 3, 1, 1, 2, 2, 8, 8, 3, 3]
     scratch += [dma((n,)) for n in sems]
     anywhere = pl.BlockSpec(memory_space=pltpu.HBM)
     inside = pl.BlockSpec(memory_space=pltpu.VMEM)

time: 52.4 us -> 50.8 us (0.969)
  the two profiles are of different devices: /device:TPU:1 before, /device:TPU:2 now
where the time goes in v3:
time: 50.8 us; the launch traced here: 50.7 us
  Pallas kernels  48.6 us (96%)
  local copies, waits for them, and re-layouts  1.52 us (3%)
  between operations  0.64 us (1%)
    pallas_call x1, Pallas kernels, shards(): pl.pallas_call(kernel, out_shape=(pltpu.VMEM((ROWS, WINDOW), BF16), pltpu...  48.6 us
    unnamed x2, local copies, waits for them, and re-layouts  1.52 us

profile of v3, /device:TPU:2, one launch (start us, length us, event | category | flops | bytes accessed | tf_op | source)
XLA Modules:
  0.0 50.7 jit_solution(6847939361689319369)
XLA Ops:
  0.6 48.6 %shard_map.59 = (bf16[104,4096]{1,0:T(8,128)(2,1)S(1)}, f32[4,2048]{1,0:T(4,128)S(1)}) custom-call(bf16[768,2048]{1,0:T(8,128)(2,1)} %calib.1, bf16[104,4096]{1,0:T(8,128)(2,1)} %weights.1, f32[64,256]{1,0:T(8,128)} %bitcast.2, s32[64,104]{1,0:T(8,128)} %bitcast.3), custom_call_target="tpu_custom_call" | custom-call | flops 2000000000 | bytes 8000000 | tf_op jit(solution)/shard_map/pallas_call | solution.py:621
  49.2 0.9 %copy.8 = bf16[104,4096]{1,0:T(8,128)(2,1)} copy(bf16[104,4096]{1,0:T(8,128)(2,1)S(1)} %get-tuple-element.2) | data formatting | bytes 1703936
  50.1 0.6 %copy.9 = f32[4,2048]{1,0:T(4,128)} copy(f32[4,2048]{1,0:T(4,128)S(1)} %get-tuple-element.3) | data formatting | bytes 65536

commit v4 on v3

--- a/solution.py
+++ b/solution.py
@@ -179,12 +179,16 @@
 
     @pl.when(owner)
     def _():
+        for k in (2, 1, 3):
+            scatter(0, k).start()
         for a in range(2):
-            for k in (2, 1, 3):
-                scatter(a, k).start()
             for u in range(2):
                 across_owner(a, u).start()
         swap_p.start()
+        for k in range(1, NX):
+            scatter(0, k).wait_send()
+        for k in (2, 1, 3):
+            scatter(1, k).start()
 
     load_x.wait()
     swap_x.start()
@@ -244,9 +248,8 @@
 
     @pl.when(owner)
     def _():
-        for a in range(2):
-            for k in range(1, NX):
-                scatter(a, k).wait_send()
+        for k in range(1, NX):
+            scatter(1, k).wait_send()
         for a in range(2):
             for k in (2, 1, 3):
                 for u in range(2):
@@ -583,6 +586,17 @@
         for n in range(2):
             over_x(g, n).wait_send()
         between(g, half).wait_send()
+
+
+def finish(pruned, gram, pruned_out, gram_out, sem):
+    copies = [
+        pltpu.make_async_copy(pruned, pruned_out, sem.at[0]),
+        pltpu.make_async_copy(gram, gram_out, sem.at[1]),
+    ]
+    for copy in copies:
+        copy.start()
+    for copy in copies:
+        copy.wait()
 
 
 def shards(calib_inputs, weights, inverse_chol, keep_pattern):
@@ -618,7 +632,7 @@
     scratch += [dma((n,)) for n in sems]
     anywhere = pl.BlockSpec(memory_space=pltpu.HBM)
     inside = pl.BlockSpec(memory_space=pltpu.VMEM)
-    return pl.pallas_call(
+    results = pl.pallas_call(
         kernel,
         out_shape=(
             pltpu.VMEM((ROWS, WINDOW), BF16),
@@ -632,6 +646,16 @@
         ),
         cost_estimate=pl.CostEstimate(flops=2 * 10**9, bytes_accessed=8 * 10**6, transcendentals=0),
     )(*[pltpu.with_memory_space_constraint(v, pltpu.HBM) for v in (calib_inputs, weights, inverse_chol.T, keep_pattern.T)])
+    return pl.pallas_call(
+        finish,
+        out_shape=(
+            jax.ShapeDtypeStruct((ROWS, WINDOW), BF16),
+            jax.ShapeDtypeStruct((PANEL_W // (NZ * NY * NC), FEAT), F32),
+        ),
+        in_specs=[inside, inside],
+        out_specs=(anywhere, anywhere),
+        scratch_shapes=[dma((2,))],
+    )(*[pltpu.with_memory_space_constraint(value, pltpu.VMEM) for value in results])
 
 
 def solution(mesh):

time: 50.8 us -> 50 us (0.984)
  the two profiles are of different devices: /device:TPU:2 before, /device:TPU:4 now
where the time goes in v4:
time: 50 us; the launch traced here: 49.9 us
  Pallas kernels  49.3 us (99%)
  between operations  0.64 us (1%)
    pallas_call x1, Pallas kernels, shards(): pl.pallas_call(kernel, out_shape=(pltpu.VMEM((ROWS, WINDOW), BF16), pltpu...  48.4 us

profile of v4, /device:TPU:4, one launch (start us, length us, event | category | flops | bytes accessed | tf_op | source)
XLA Modules:
  0.0 49.9 jit_solution(10731178470131616126)
XLA Ops:
  0.6 48.4 %shard_map.59 = (bf16[104,4096]{1,0:T(8,128)(2,1)S(1)}, f32[4,2048]{1,0:T(4,128)S(1)}) custom-call(bf16[768,2048]{1,0:T(8,128)(2,1)} %calib.1, bf16[104,4096]{1,0:T(8,128)(2,1)} %weights.1, f32[64,256]{1,0:T(8,128)} %bitcast.2, s32[64,104]{1,0:T(8,128)} %bitcast.3), custom_call_target="tpu_custom_call" | custom-call | flops 2000000000 | bytes 8000000 | tf_op jit(solution)/shard_map/pallas_call | solution.py:635
  49.0 0.9 %shard_map.60 = (bf16[104,4096]{1,0:T(8,128)(2,1)}, f32[4,2048]{1,0:T(4,128)}) custom-call(bf16[104,4096]{1,0:T(8,128)(2,1)S(1)} %get-tuple-element.4.pruned, f32[4,2048]{1,0:T(4,128)S(1)} %get-tuple-element.5.gram), custom_call_target="tpu_custom_call" | custom-call | tf_op jit(solution)/shard_map/pallas_call | solution.py:649

commit v5 on v4

--- a/solution.py
+++ b/solution.py
@@ -64,7 +64,7 @@
 def kernel(
     calib, weights, inverse, pattern,
     pruned, gram,
-    xv, pv, wv, kv, iv, ipeer, blk, qv, hv, gv, msend, mrecv, ysend, yrecv,
+    xv, pv, wv, kv, iv, ipeer, blk, qv, hv, gv, msend, mrecv, ysend, ypack, yrecv,
     wpad, kpad, dg, ct, av, et, eh, el, po, pt,
     lsem, isem, s1s, s1r, hcs, hcr, s2s, s2r,
     qys, qyr, qzs, qzr, qxs, qxr, qcs, qcr, hys, hyr, hzs, hzr, hxs, hxr, hs, hr,
@@ -516,8 +516,20 @@
         summed = jnp.concatenate(tiles[4 * tile : 4 * tile + 4], axis=1)
         for yd in range(NY):
             ysend[yd, tile * 4 : tile * 4 + 4, :] = summed[yd * 4 : yd * 4 + 4, :]
+    for yd in range(NY):
+        value = ysend[yd]
+        most = jnp.abs(value[:, 0:128])
+        for i in range(1, 4):
+            most = jnp.maximum(most, jnp.abs(value[:, 128 * i : 128 * i + 128]))
+        most = jnp.max(most, axis=0, keepdims=True)
+        power = jnp.ceil(jnp.log2(jnp.maximum(most, 1e-30)))
+        up = jnp.exp2(-power) * SUM_MAX
+        for i in range(4):
+            code = jnp.round(value[:, 128 * i : 128 * i + 128] * up)
+            ypack[yd, i] = code.astype(jnp.int32).astype(jnp.int16)
+        ypack[yd, 4] = jnp.broadcast_to(power, (16, 128)).astype(jnp.int32).astype(jnp.int16)
     r_y = [
-        remote(ysend.at[yp(k)], yrecv.at[k - 1], rys.at[k - 1], ryr.at[k - 1], at(y=yp(k)))
+        remote(ypack.at[yp(k)], yrecv.at[k - 1], rys.at[k - 1], ryr.at[k - 1], at(y=yp(k)))
         for k in range(1, NY)
     ]
     for copy in r_y:
@@ -545,7 +557,12 @@
 
     for copy in r_y:
         copy.wait_recv()
-    total = ysend[y] + yrecv[0] + yrecv[1] + yrecv[2]
+    total = ysend[y]
+    for k in range(NY - 1):
+        down = jnp.exp2(yrecv[k, 4].astype(jnp.int32).astype(F32)) * (1.0 / SUM_MAX)
+        total = total + jnp.concatenate(
+            [yrecv[k, i].astype(jnp.int32).astype(F32) * down for i in range(4)], axis=1
+        )
     total = total * (2.0 / (TOK * NZ * NY * NC))
     for tile in range(4):
         gram[:, tile * 512 : tile * 512 + 512] = total[tile * 4 : tile * 4 + 4, :]
@@ -616,7 +633,8 @@
         vmem((7, 17, 16, 128), jnp.int16),
         vmem((8, 17, 16, 128), jnp.int16),
         vmem((NY, 16, 512), F32),
-        vmem((NY - 1, 16, 512), F32),
+        vmem((NY, 5, 16, 128), jnp.int16),
+        vmem((NY - 1, 5, 16, 128), jnp.int16),
         vmem((LANES, PANEL_W), F32),
         vmem((LANES, LANES), F32),
         vmem((PANEL_W // BLOCK, BLOCK, 128), F32),

time: 50 us -> 50 us (level)
  no operation moved by 1% of the time
where the time goes in v5:
time: 50 us; the launch traced here: 49.8 us
  Pallas kernels  49.2 us (98%)
  between operations  0.64 us (1%)
    pallas_call x1, Pallas kernels, shards(): pl.pallas_call(kernel, out_shape=(pltpu.VMEM((ROWS, WINDOW), BF16), pltpu...  48.3 us

profile of v5, /device:TPU:4, one launch (start us, length us, event | category | flops | bytes accessed | tf_op | source)
XLA Modules:
  0.0 49.8 jit_solution(15410544898786657431)
XLA Ops:
  0.6 48.3 %shard_map.59 = (bf16[104,4096]{1,0:T(8,128)(2,1)S(1)}, f32[4,2048]{1,0:T(4,128)S(1)}) custom-call(bf16[768,2048]{1,0:T(8,128)(2,1)} %calib.1, bf16[104,4096]{1,0:T(8,128)(2,1)} %weights.1, f32[64,256]{1,0:T(8,128)} %bitcast.2, s32[64,104]{1,0:T(8,128)} %bitcast.3), custom_call_target="tpu_custom_call" | custom-call | flops 2000000000 | bytes 8000000 | tf_op jit(solution)/shard_map/pallas_call | solution.py:653
  48.9 0.9 %shard_map.60 = (bf16[104,4096]{1,0:T(8,128)(2,1)}, f32[4,2048]{1,0:T(4,128)}) custom-call(bf16[104,4096]{1,0:T(8,128)(2,1)S(1)} %get-tuple-element.4.pruned, f32[4,2048]{1,0:T(4,128)S(1)} %get-tuple-element.5.gram), custom_call_target="tpu_custom_call" | custom-call | tf_op jit(solution)/shard_map/pallas_call | solution.py:667
